TPU v7x, 32 devices: a whole 2x2x4 slice. The times are simulated.
32 devices in a mesh: clip: 4 (over y, x), tm: 8 (over z, core).
Axes of the slice: x: 2, y: 2, z: 4, core: 2. Of those that a mesh axis runs over, the one named last changes fastest.
Arguments:
- x_inner: bfloat16 [32, 192, 2048], P(('clip', 'tm')), parts along dimension 0, may hold values from -6 to 6
- bc_inputs: bfloat16 [32, 192, 256], P(('clip', 'tm')), parts along dimension 0, may hold values from -2 to 2
- step_raw: bfloat16 [32, 192, 64], P(('clip', 'tm')), parts along dimension 0, may hold values from -5 to 5
- decay_rate: float32 [2, 32], replicated, may hold values from 0.002 to 0.3
- skip_gain: float32 [32], replicated, may hold values from 0.1 to 1.9
- w_out: bfloat16 [2048, 1024], P('tm'), may hold values from -0.125 to 0.125
- grad_out: bfloat16 [32, 192, 1024], P(('clip', 'tm')), parts along dimension 0, may hold values from -6 to 6
Outputs:
- mixed_out: bfloat16 [32, 192, 1024], P(('clip', 'tm')), parts along dimension 0
- grad_inner: bfloat16 [32, 192, 2048], P(('clip', 'tm')), parts along dimension 0
- grad_bc: bfloat16 [32, 192, 256], P(('clip', 'tm')), parts along dimension 0
- grad_step: bfloat16 [32, 192, 64], P(('clip', 'tm')), parts along dimension 0
- grad_w_out: float32 [8192, 1024], P(('clip', 'tm')), parts along dimension 0
There are 4 independent parts, one for each index of `clip`. A program takes and returns all parts, laid end to end along the dimension named above; an argument that names none is the same for every part. Nothing has to cross between parts.
All inputs are finite; a program needn't handle non-finite values.
Results may differ from a plain program's by a relative error of at most 0.022.
Values may be sent and summed in bfloat16 or wider, within the bound.
A program may use at most 128 MiB of HBM per device.

v0:
```python
import functools

import jax
import jax.numpy as jnp
from jax import lax
from jax.experimental import pallas as pl
from jax.experimental.pallas import tpu as pltpu
from jax.sharding import PartitionSpec as P

F32 = jnp.float32
BF16 = jnp.bfloat16
HIGH = lax.Precision.HIGHEST
LANES = 128


def iota(shape, dim):
    return lax.broadcasted_iota(jnp.int32, shape, dim)


def mm(a, b, ca=1, cb=0, precision=None):
    return lax.dot_general(
        a, b, (((ca,), (cb,)), ((), ())), precision=precision, preferred_element_type=F32
    )


def softplus(raw):
    return jnp.maximum(raw, 0.0) + jnp.log(1.0 + jnp.exp(-jnp.abs(raw)))


def picker(rows, base, count):
    r, c = iota((rows, LANES), 0), iota((rows, LANES), 1)
    return jnp.where((r == c + base) & (c < count), 1.0, 0.0).astype(BF16)


def steps_of(raw_bf, pick, decay_row, mask):
    raw = mm(raw_bf, pick)
    step = softplus(raw)
    cum = mm(mask, -step * decay_row, precision=HIGH)
    return raw, step, cum, step.T, cum.T


def weights_of(head, cum, cum_t, step_t):
    gap = cum[:, head : head + 1] - cum_t[head : head + 1, :]
    return jnp.exp(jnp.minimum(gap, 0.0)) * step_t[head : head + 1, :]


def step_grad(row_sums, col_sums_t, raw, step, decay_row, mask):
    col_sums = col_sums_t.T
    later = mm(mask, row_sums - col_sums, 0, 0, precision=HIGH)
    grad = col_sums / step - decay_row * later
    return grad / (1.0 + jnp.exp(-raw))


def forward_kernel(nheads, chunk, x_ref, bc_ref, raw_ref, decay_ref, out_ref):
    length = x_ref.shape[0]
    n = bc_ref.shape[1] // 4
    mask = jnp.where(iota((length, length), 0) >= iota((length, length), 1), 1.0, 0.0)
    pick = picker(raw_ref.shape[1], 0, nheads)
    _, _, cum, step_t, cum_t = steps_of(raw_ref[...], pick, decay_ref[0:1, :], mask)
    gram = mm(bc_ref[:, n : 2 * n], bc_ref[:, :n], 1, 1) * mask
    first = iota((length, LANES), 1) < LANES // 2
    for pair in range(nheads // 2):
        xp = x_ref[:, pair * LANES : (pair + 1) * LANES]
        ys = []
        for e in range(2):
            m = gram * weights_of(2 * pair + e, cum, cum_t, step_t)
            ys.append(mm(m.astype(BF16), xp))
        at = pair * LANES
        out_ref[at // chunk, :, at % chunk : at % chunk + LANES] = jnp.where(
            first, ys[0], ys[1]
        ).astype(BF16)


def backward_kernel(
    nheads, chunk, x_ref, bc_ref, raw_ref, decay_ref, dy_ref, dx_ref, dbc_ref, draw_ref
):
    length = x_ref.shape[0]
    n = bc_ref.shape[1] // 4
    mask = jnp.where(iota((length, length), 0) >= iota((length, length), 1), 1.0, 0.0)
    pick = picker(raw_ref.shape[1], 0, nheads)
    decay_row = decay_ref[0:1, :]
    raw, step, cum, step_t, cum_t = steps_of(raw_ref[...], pick, decay_row, mask)
    b, c = bc_ref[:, :n], bc_ref[:, n : 2 * n]
    gram = mm(c, b, 1, 1) * mask
    lane = iota((length, LANES), 1)
    first = lane < LANES // 2
    sub = iota((LANES, length), 0)
    dgram = jnp.zeros((length, length), F32)
    row_sums = jnp.zeros((length, LANES), F32)
    col_sums = jnp.zeros((LANES, length), F32)
    for pair in range(nheads // 2):
        at = pair * LANES
        xp = x_ref[:, at : at + LANES]
        gp = dy_ref[at // chunk, :, at % chunk : at % chunk + LANES]
        dxs = []
        for e in range(2):
            head = 2 * pair + e
            ls = weights_of(head, cum, cum_t, step_t)
            m = gram * ls
            ge = jnp.where(first if e == 0 else ~first, gp, jnp.zeros_like(gp))
            dm = mm(ge, xp, 1, 1)
            dgram = dgram + dm * ls
            w = dm * m
            row_sums = jnp.where(lane == head, jnp.sum(w, axis=1, keepdims=True), row_sums)
            col_sums = jnp.where(sub == head, jnp.sum(w, axis=0, keepdims=True), col_sums)
            dxs.append(mm(m.astype(BF16), gp, 0, 0))
        dx_ref[:, at : at + LANES] = jnp.where(first, dxs[0], dxs[1]).astype(BF16)
    draw = step_grad(row_sums, col_sums, raw, step, decay_row, mask)
    draw_ref[...] = draw[:, :nheads].astype(BF16)
    dgb = (dgram * mask).astype(BF16)
    dbc_ref[:, :n] = mm(dgb, c, 0, 0).astype(BF16)
    dbc_ref[:, n:] = mm(dgb, b).astype(BF16)


def temporal_kernel(
    nheads, mine, group,
    base_ref, decay_ref, skip_ref, x_ref, go_ref, aux_ref, w_ref,
    dx_ref, part_ref, daux_ref, gw_ref, mixed_ref,
):
    frames, patches, width = x_ref.shape
    n = (aux_ref.shape[2] - nheads) // 2
    base = base_ref[0]
    rows = frames * group
    ri, ci = iota((rows, rows), 0), iota((rows, rows), 1)
    mask = jnp.where((ri % group == ci % group) & (ri >= ci), 1.0, 0.0)
    pick = picker(nheads, base, mine)
    lane = iota((rows, LANES), 1)
    sub = iota((LANES, rows), 0)
    first = lane < LANES // 2
    lane1 = iota((1, LANES), 1)
    decay_row = jnp.zeros((1, LANES), F32)
    for h in range(mine):
        decay_row = jnp.where(lane1 == h, decay_ref[1, base + h], decay_row)
    w = w_ref[...]
    go = go_ref[...].reshape(frames * patches, go_ref.shape[2])
    carried = mm(go, w, 1, 1).astype(BF16).reshape(frames, patches, width)
    for part in range(patches // group):
        sl = slice(part * group, (part + 1) * group)
        x = x_ref[:, sl, :].reshape(rows, width)
        g = carried[:, sl, :].reshape(rows, width)
        aux = aux_ref[:, sl, :].reshape(rows, aux_ref.shape[2])
        b, c = aux[:, :n], aux[:, n : 2 * n]
        raw, step, cum, step_t, cum_t = steps_of(aux[:, 2 * n :], pick, decay_row, mask)
        gram = mm(c, b, 1, 1) * mask
        dgram = jnp.zeros((rows, rows), F32)
        row_sums = jnp.zeros((rows, LANES), F32)
        col_sums = jnp.zeros((LANES, rows), F32)
        for pair in range(mine // 2):
            at = pair * LANES
            xp, gp = x[:, at : at + LANES], g[:, at : at + LANES]
            ys, dxs = [], []
            for e in range(2):
                head = 2 * pair + e
                ls = weights_of(head, cum, cum_t, step_t)
                m = gram * ls
                mb = m.astype(BF16)
                ge = jnp.where(first if e == 0 else ~first, gp, jnp.zeros_like(gp))
                dm = mm(ge, xp, 1, 1)
                dgram = dgram + dm * ls
                wm = dm * m
                row_sums = jnp.where(lane == head, jnp.sum(wm, axis=1, keepdims=True), row_sums)
                col_sums = jnp.where(sub == head, jnp.sum(wm, axis=0, keepdims=True), col_sums)
                ys.append(mm(mb, xp))
                dxs.append(mm(mb, gp, 0, 0))
            skip = jnp.where(
                lane1 < LANES // 2, skip_ref[base + 2 * pair], skip_ref[base + 2 * pair + 1]
            )
            y = jnp.where(first, ys[0], ys[1]) + skip * xp.astype(F32)
            dx = jnp.where(first, dxs[0], dxs[1]) + skip * gp.astype(F32)
            mixed_ref[:, sl, at : at + LANES] = y.astype(BF16).reshape(frames, group, LANES)
            dx_ref[:, sl, at : at + LANES] = dx.astype(BF16).reshape(frames, group, LANES)
        draw = step_grad(row_sums, col_sums, raw, step, decay_row, mask)
        placed = mm(draw.astype(BF16), pick, 1, 1)
        dgb = (dgram * mask).astype(BF16)
        shape = lambda v: v.astype(BF16).reshape(frames, group, v.shape[1])
        daux_ref[:, sl, :n] = shape(mm(dgb, c, 0, 0))
        daux_ref[:, sl, n : 2 * n] = shape(mm(dgb, b))
        daux_ref[:, sl, 2 * n :] = shape(placed)
    mixed = mixed_ref[...].reshape(frames * patches, width)
    part_ref[...] = mm(mixed, w).astype(BF16).reshape(part_ref.shape)

    @pl.when(pl.program_id(0) == 0)
    def _():
        gw_ref[...] = jnp.zeros_like(gw_ref)

    gw_ref[...] += mm(mixed, go, 0, 0)


VMEM = pl.BlockSpec(memory_space=pltpu.VMEM)
SMEM = pl.BlockSpec(memory_space=pltpu.SMEM)
PARAMS = pltpu.CompilerParams(vmem_limit_bytes=48 * 1024 * 1024)


def on_device(x_inner, bc_inputs, step_raw, decay_rate, skip_gain, w_out, grad_out, tm):
    nheads = skip_gain.shape[0]
    _, patches, inner = x_inner.shape
    n2 = bc_inputs.shape[2] // 2
    model = w_out.shape[1]
    chunk = inner // tm
    mine = nheads // tm
    x, bc, raw = x_inner[0], bc_inputs[0], step_raw[0]
    decay_pad = jnp.pad(decay_rate, ((0, 0), (0, LANES - nheads)))
    aux = jnp.concatenate([bc[:, n2:], raw[:, nheads:]], axis=1)
    aux_all = lax.all_gather(aux, "tm", axis=0)
    go_all = lax.all_gather(grad_out[0], "tm", axis=0)

    spatial = pl.pallas_call(
        functools.partial(forward_kernel, nheads, chunk),
        out_shape=jax.ShapeDtypeStruct((tm, patches, chunk), BF16),
        in_specs=[VMEM] * 4,
        out_specs=VMEM,
        compiler_params=PARAMS,
        name="spatial_forward",
        cost_estimate=pl.CostEstimate(
            flops=6 * patches * patches * inner, bytes_accessed=4 * patches * inner,
            transcendentals=patches * patches * nheads,
        ),
    )(x, bc, raw, decay_pad)
    spatial_here = lax.all_to_all(spatial, "tm", 0, 0, tiled=True)

    rows = 32
    block = lambda width: pl.BlockSpec((tm, rows, width), lambda i: (0, i, 0))
    whole = pl.BlockSpec((chunk, model), lambda i: (0, 0))
    auxw = aux.shape[1]
    base = (lax.axis_index("tm") * mine).astype(jnp.int32).reshape(1)
    grad_here, partial_out, partial_aux, grad_w = pl.pallas_call(
        functools.partial(temporal_kernel, nheads, mine, 16),
        grid=(patches // rows,),
        out_shape=(
            jax.ShapeDtypeStruct((tm, patches, chunk), BF16),
            jax.ShapeDtypeStruct((tm, patches, model), BF16),
            jax.ShapeDtypeStruct((tm, patches, auxw), BF16),
            jax.ShapeDtypeStruct((chunk, model), F32),
        ),
        in_specs=[SMEM, SMEM, SMEM, block(chunk), block(model), block(auxw), whole],
        out_specs=(block(chunk), block(model), block(auxw), whole),
        scratch_shapes=[pltpu.VMEM((tm, rows, chunk), BF16)],
        compiler_params=PARAMS,
        name="temporal",
        cost_estimate=pl.CostEstimate(
            flops=6 * tm * patches * chunk * model, bytes_accessed=8 * tm * patches * model,
            transcendentals=tm * patches * 128 * mine,
        ),
    )(base, decay_rate, skip_gain, spatial_here, go_all, aux_all, w_out)

    grad_spatial = lax.all_to_all(grad_here, "tm", 0, 0, tiled=True)
    mixed_out = lax.psum_scatter(partial_out, "tm", scatter_dimension=0, tiled=True)
    aux_back = lax.psum_scatter(partial_aux, "tm", scatter_dimension=0, tiled=True)[0]

    grad_x, grad_bc_s, grad_raw_s = pl.pallas_call(
        functools.partial(backward_kernel, nheads, chunk),
        out_shape=(
            jax.ShapeDtypeStruct((patches, inner), BF16),
            jax.ShapeDtypeStruct((patches, n2), BF16),
            jax.ShapeDtypeStruct((patches, nheads), BF16),
        ),
        in_specs=[VMEM] * 5,
        out_specs=(VMEM, VMEM, VMEM),
        compiler_params=PARAMS,
        name="spatial_backward",
        cost_estimate=pl.CostEstimate(
            flops=12 * patches * patches * inner, bytes_accessed=6 * patches * inner,
            transcendentals=patches * patches * nheads,
        ),
    )(x, bc, raw, decay_pad, grad_spatial)
    grad_bc = jnp.concatenate([grad_bc_s, aux_back[:, :n2]], axis=1)
    grad_step = jnp.concatenate([grad_raw_s, aux_back[:, n2:]], axis=1)
    return (mixed_out, grad_x[None], grad_bc[None], grad_step[None], grad_w)


def solution(mesh):
    in_specs = (
        P(("clip", "tm"), None, None),
        P(("clip", "tm"), None, None),
        P(("clip", "tm"), None, None),
        P(),
        P(),
        P("tm", None),
        P(("clip", "tm"), None, None),
    )
    out_specs = (
        P(("clip", "tm"), None, None),
        P(("clip", "tm"), None, None),
        P(("clip", "tm"), None, None),
        P(("clip", "tm"), None, None),
        P(("clip", "tm"), None),
    )
    return jax.shard_map(
        functools.partial(on_device, tm=mesh.shape["tm"]),
        mesh=mesh, in_specs=in_specs, out_specs=out_specs, check_vma=False,
    )
```

profile of v0, /device:TPU:0, one launch (start us, length us, event | category | flops | bytes accessed | tf_op | source)
XLA Modules:
  0.0 179.6 jit_solution(15279057794066369154)
XLA Ops:
  7.2 0.0 copy-start.1
  7.2 0.0 all-gather.4.cloned.1.call-start
  7.2 0.7 all-gather.4.cloned.1.call-update
  7.9 0.9 copy.14
  8.8 0.7 pad.4.decay_ref
  9.5 0.0 copy-start
  9.5 0.9 copy-done
  10.4 0.0 copy-start.3
  10.4 1.1 copy-done.3
  11.5 0.0 copy-start.2
  11.5 0.0 copy-start.5
  11.5 0.0 copy-start.6
  11.5 3.2 %spatial_forward.1 = bf16[8,192,256]{2,1,0:T(8,128)(2,1)} custom-call(bf16[192,2048]{1,0:T(8,128)(2,1)S(1)} %bitcast.18, bf16[192,256]{1,0:T(8,128)(2,1)S(1)} %bitcast.15, bf16[192,64]{1,0:T(8,128)(2,1)S(1)} %bitcast.12, f32[2,128]{1,0:T(2,128)S(1)} %pad.4.decay_ref), custom_call_target="tpu_custom_call" | custom-call | flops 452984832 | bytes 1572864 | tf_op jit(solution)/shard_map/spatial_forward/pallas_call | solution.py:207
  14.8 6.3 %all-to-all-start = ((bf16[8,192,256]{2,1,0:T(8,128)(2,1)}), bf16[8,192,256]{2,1,0:T(8,128)(2,1)S(1)}, u32[]{:S(2)}, u32[]{:S(2)}) async-start(bf16[8,192,256]{2,1,0:T(8,128)(2,1)} %spatial_forward.1), calls=%async_computation | async-start | bytes 1572864 | tf_op jit(solution)/shard_map/all_to_all | solution.py:219
  21.1 0.0 reduce-scatter.5.cloned.1.call-start
  21.1 0.0 copy-done.1
  21.1 0.1 slice.17
  21.3 0.1 copy.15
  21.4 51.8 %all-gather.1 = bf16[8,192,160]{1,2,0:T(8,128)(2,1)S(1)} all-gather(bf16[1,192,160]{1,2,0:T(8,128)(2,1)S(1)} %copy.15), channel_id=2, replica_groups=mesh['clip'=4,'tm'=8] {'tm'}, dimensions={0}, use_global_device_ids=true | all-gather | bytes 552960 | tf_op jit(solution)/shard_map/all_gather | solution.py:204
  73.2 0.3 copy.16.aux_ref
  73.5 0.0 all-to-all-done.x_ref
  73.5 0.0 all-gather.4.cloned.1.call-done.go_ref
  73.5 0.0 copy-done.2
  73.6 0.0 copy-done.5
  73.6 0.0 copy-done.6
  73.6 21.0 %temporal.1 = (bf16[8,192,256]{2,1,0:T(8,128)(2,1)}, bf16[8,192,1024]{2,1,0:T(8,128)(2,1)}, bf16[8,192,160]{2,1,0:T(8,128)(2,1)}, f32[256,1024]{1,0:T(8,128)}) custom-call(s32[1]{0:T(128)} %bitcast.base_ref, f32[2,32]{1,0:T(2,128)S(1)} %copy-done.2, f32[32]{0:T(128)S(1)} %copy-done.6, bf16[8,192,256]{2,1,0:T(8,128)(2,1)S(1)} %all-to-all-done.x_ref, ...), custom_call_target="tpu_custom_call" | custom-call | flops 2415919104 | bytes 12582912 | tf_op jit(solution)/shard_map/temporal/pallas_call | solution.py:226
  94.6 0.0 copy-start.4
  94.6 0.0 reduce-scatter.5.cloned.1.call-update
  94.7 0.0 reduce-scatter.3.cloned.1.call-start
  94.7 0.7 reduce-scatter.3.cloned.1.call-update
  95.4 4.0 %all-to-all-start.1 = ((bf16[8,192,256]{2,1,0:T(8,128)(2,1)}), bf16[8,192,256]{2,1,0:T(8,128)(2,1)S(1)}, u32[]{:S(2)}, u32[]{:S(2)}) async-start(bf16[8,192,256]{2,1,0:T(8,128)(2,1)} %get-tuple-element.13), calls=%async_computation.2 | async-start | bytes 1572864 | tf_op jit(solution)/shard_map/all_to_all | solution.py:246
  99.4 29.9 %reduce-scatter.5.cloned.1.call-done = bf16[1,192,160]{2,1,0:T(8,128)(2,1)} async-done(((bf16[8,192,160]{2,1,0:T(8,128)(2,1)}), bf16[1,192,160]{2,1,0:T(8,128)(2,1)}) %reduce-scatter.5.cloned.1.call-update) | async-done | bytes 61456 | tf_op jit(solution)/shard_map/reduce_scatter | solution.py:248
  129.3 0.8 slice.19
  130.1 0.8 slice.18
  130.9 0.0 all-to-all-done.1.dy_ref
  130.9 0.0 copy-done.4
  131.0 8.3 %spatial_backward.1 = (bf16[192,2048]{1,0:T(8,128)(2,1)}, bf16[192,128]{1,0:T(8,128)(2,1)S(1)}, bf16[192,32]{1,0:T(8,128)(2,1)S(1)}) custom-call(bf16[192,2048]{1,0:T(8,128)(2,1)S(1)} %bitcast.19, bf16[192,256]{1,0:T(8,128)(2,1)S(1)} %bitcast.17, bf16[192,64]{1,0:T(8,128)(2,1)S(1)} %bitcast.14, f32[2,128]{1,0:T(2,128)S(1)} %pad.4.decay_ref, ...), custom_call_target="tpu_custom_call" | custom-call | flops 905969664 | bytes 2359296 | tf_op jit(solution)/shard_map/spatial_backward/pallas_call | solution.py:250
  139.3 0.1 maximum_bitcast_fusion.2
  139.4 0.7 copy.17
  140.1 0.7 maximum_bitcast_fusion.1
  140.8 32.3 %reduce-scatter.3.cloned.1.call-done = bf16[1,192,1024]{2,1,0:T(8,128)(2,1)} async-done(((bf16[8,192,1024]{2,1,0:T(8,128)(2,1)}), bf16[1,192,1024]{2,1,0:T(8,128)(2,1)}) %reduce-scatter.3.cloned.1.call-update) | async-done | bytes 393232 | tf_op jit(solution)/shard_map/reduce_scatter | solution.py:247
  (2 shorter events, 0.0 us)
Async XLA Ops:
  7.2 14.0 %copy-start.1 = (bf16[1,192,256]{2,1,0:T(8,128)(2,1)S(1)}, bf16[1,192,256]{2,1,0:T(8,128)(2,1)}, u32[]{:S(2)}) copy-start(bf16[1,192,256]{2,1,0:T(8,128)(2,1)} %param.8) | copy-start | bytes 294916
  7.2 66.4 %all-gather.4.cloned.1.call-start = ((), (), s32[]{:S(2)}) async-start(), calls=%async_computation.4 | async-start | bytes 3538944 | tf_op jit(solution)/shard_map/all_gather | solution.py:205
  9.5 0.9 copy-start
  10.4 1.1 copy-start.3
  11.5 62.0 %copy-start.2 = (f32[2,32]{1,0:T(2,128)S(1)}, f32[2,32]{1,0:T(2,128)}, u32[]{:S(2)}) copy-start(f32[2,32]{1,0:T(2,128)} %decay_ref.1) | copy-start | bytes 772
  11.5 62.1 %copy-start.5 = (bf16[256,1024]{1,0:T(8,128)(2,1)S(1)}, bf16[256,1024]{1,0:T(8,128)(2,1)}, u32[]{:S(2)}) copy-start(bf16[256,1024]{1,0:T(8,128)(2,1)} %w_ref.1) | copy-start | bytes 1572868
  11.5 62.1 %copy-start.6 = (f32[32]{0:T(128)S(1)}, f32[32]{0:T(128)}, u32[]{:S(2)}) copy-start(f32[32]{0:T(128)} %skip_ref.1) | copy-start | bytes 388
  14.8 58.8 %all-to-all-start = ((bf16[8,192,256]{2,1,0:T(8,128)(2,1)}), bf16[8,192,256]{2,1,0:T(8,128)(2,1)S(1)}, u32[]{:S(2)}, u32[]{:S(2)}) async-start(bf16[8,192,256]{2,1,0:T(8,128)(2,1)} %spatial_forward.1), calls=%async_computation | async-start | bytes 1572864 | tf_op jit(solution)/shard_map/all_to_all | solution.py:219
  21.1 108.3 %reduce-scatter.5.cloned.1.call-start = ((), (), s32[]{:S(2)}) async-start(), calls=%async_computation.6 | async-start | bytes 884736 | tf_op jit(solution)/shard_map/reduce_scatter | solution.py:248
  94.6 36.3 %copy-start.4 = (bf16[1,192,2048]{2,1,0:T(8,128)(2,1)S(1)}, bf16[1,192,2048]{2,1,0:T(8,128)(2,1)}, u32[]{:S(2)}) copy-start(bf16[1,192,2048]{2,1,0:T(8,128)(2,1)} %param.7) | copy-start | bytes 2359300
  94.7 78.4 %reduce-scatter.3.cloned.1.call-start = ((), (), s32[]{:S(2)}) async-start(), calls=%async_computation.5 | async-start | bytes 3538944 | tf_op jit(solution)/shard_map/reduce_scatter | solution.py:247
  95.4 35.6 %all-to-all-start.1 = ((bf16[8,192,256]{2,1,0:T(8,128)(2,1)}), bf16[8,192,256]{2,1,0:T(8,128)(2,1)S(1)}, u32[]{:S(2)}, u32[]{:S(2)}) async-start(bf16[8,192,256]{2,1,0:T(8,128)(2,1)} %get-tuple-element.13), calls=%async_computation.2 | async-start | bytes 1572864 | tf_op jit(solution)/shard_map/all_to_all | solution.py:246
Sparse Core Ops, SparseCore 0:
  9.7 62.2 all-gather.3
  94.8 34.5 reduce-scatter.4
  132.3 40.6 reduce-scatter.2
where the time goes:
time: 180 us
  waiting for transfers between devices  63.6 us (35%)
  blocking collectives  51.8 us (29%)
  Pallas kernels  32.6 us (18%)
  between operations  13.9 us (8%)
  starting transfers between devices  10.5 us (6%)
  local copies, waits for them, and re-layouts  6.44 us (4%)
    all_gather x1, blocking collectives, on_device(): aux_all = lax.all_gather(aux, 'tm', axis=0)  51.8 us
    reduce_scatter x1, waiting for transfers between devices, on_device(): lax.psum_scatter(partial_out, 'tm', scatter_dimension=0, tiled=True)  32.3 us
    reduce_scatter x1, waiting for transfers between devices, on_device(): lax.psum_scatter(partial_aux, 'tm', scatter_dimension=0, tiled=True)[0]  29.9 us
    pallas_call x1, Pallas kernels, on_device(): pl.pallas_call(functools.partial(temporal_kernel, nheads, mine, 16), grid...  21 us
    pallas_call x1, Pallas kernels, on_device(): pl.pallas_call(functools.partial(backward_kernel, nheads, chunk), out_sha...  8.35 us
    all_to_all x1, starting transfers between devices, on_device(): spatial_here = lax.all_to_all(spatial, 'tm', 0, 0, tiled=True)  6.32 us
    all_to_all x1, starting transfers between devices, on_device(): grad_spatial = lax.all_to_all(grad_here, 'tm', 0, 0, tiled=True)  4.02 us
    unnamed x17, local copies, waits for them, and re-layouts  3.72 us
  transfers between devices with their start and end apart: 5, of which 2 were waited for; matrix products, arithmetic and copies ran while one was open for 3% of the time, Pallas kernels for 6%

commit v1 on v0

--- a/solution.py
+++ b/solution.py
@@ -27,6 +27,9 @@
     return jnp.maximum(raw, 0.0) + jnp.log(1.0 + jnp.exp(-jnp.abs(raw)))
 
 
+DMA = pltpu.SemaphoreType.DMA
+
+
 def picker(rows, base, count):
     r, c = iota((rows, LANES), 0), iota((rows, LANES), 1)
     return jnp.where((r == c + base) & (c < count), 1.0, 0.0).astype(BF16)
@@ -51,9 +54,49 @@
     return grad / (1.0 + jnp.exp(-raw))
 
 
-def forward_kernel(nheads, chunk, x_ref, bc_ref, raw_ref, decay_ref, out_ref):
+def remote(src, dst, send, recv, peer):
+    return pltpu.make_async_remote_copy(
+        src_ref=src, dst_ref=dst, send_sem=send, recv_sem=recv,
+        device_id={"tm": peer}, device_id_type=pl.DeviceIdType.MESH,
+    )
+
+
+def greet_all(me, tm):
+    barrier = pltpu.get_barrier_semaphore()
+    for d in range(1, tm):
+        pl.semaphore_signal(
+            barrier, inc=1, device_id={"tm": lax.rem(me + d, tm)},
+            device_id_type=pl.DeviceIdType.MESH,
+        )
+    pl.semaphore_wait(barrier, tm - 1)
+
+
+def forward_kernel(
+    nheads, chunk, tm,
+    x_ref, bc_ref, raw_ref, decay_ref, go_ref, aux_ref,
+    here_ref, go_all, aux_all,
+    out_ref, own_sem, sp_send, sp_recv, go_send, go_recv, aux_send, aux_recv,
+):
     length = x_ref.shape[0]
     n = bc_ref.shape[1] // 4
+    me = lax.axis_index("tm")
+    core = lax.rem(me, 2)
+    partner = me + 1 - 2 * core
+    own = [
+        pltpu.make_async_copy(go_ref, go_all.at[me], own_sem.at[0]),
+        pltpu.make_async_copy(aux_ref, aux_all.at[me], own_sem.at[1]),
+    ]
+    for copy in own:
+        copy.start()
+    greet_all(me, tm)
+    gathers = ((go_ref, go_all, go_send, go_recv), (aux_ref, aux_all, aux_send, aux_recv))
+    sends = []
+    for src, dst, send, recv in gathers:
+        for d in range(tm // 2):
+            peer = partner if d == 0 else lax.rem(me + 2 * d, tm)
+            sends.append(remote(src, dst.at[me], send.at[d], recv.at[me], peer))
+            sends[-1].start()
+
     mask = jnp.where(iota((length, length), 0) >= iota((length, length), 1), 1.0, 0.0)
     pick = picker(raw_ref.shape[1], 0, nheads)
     _, _, cum, step_t, cum_t = steps_of(raw_ref[...], pick, decay_ref[0:1, :], mask)
@@ -70,10 +113,91 @@
             first, ys[0], ys[1]
         ).astype(BF16)
 
+    own.append(pltpu.make_async_copy(out_ref.at[me], here_ref.at[me], own_sem.at[2]))
+    own[-1].start()
+    for d in range(1, tm):
+        peer = lax.rem(me + d, tm)
+        sends.append(
+            remote(out_ref.at[peer], here_ref.at[me], sp_send.at[d], sp_recv.at[me], peer)
+        )
+        sends[-1].start()
+    for src, dst, send, recv in reversed(gathers):
+        for d in range(1, tm // 2):
+            got = lax.rem(me + 2 * d, tm)
+            remote(src, dst.at[got], send.at[0], recv.at[got], partner).wait_recv()
+            sends.append(
+                remote(dst.at[got], dst.at[got], send.at[tm // 2 + d], recv.at[got], partner)
+            )
+            sends[-1].start()
+    for src, dst, send, recv in gathers:
+        for d in range(tm // 2):
+            got = lax.rem(partner + 2 * d, tm)
+            remote(src, dst.at[got], send.at[0], recv.at[got], partner).wait_recv()
+    for d in range(1, tm):
+        got = lax.rem(me + d, tm)
+        remote(out_ref.at[got], here_ref.at[got], sp_send.at[d], sp_recv.at[got], got).wait_recv()
+    for copy in own:
+        copy.wait()
+    for copy in sends:
+        copy.wait_send()
+
 
 def backward_kernel(
-    nheads, chunk, x_ref, bc_ref, raw_ref, decay_ref, dy_ref, dx_ref, dbc_ref, draw_ref
+    nheads, chunk, tm,
+    x_ref, bc_ref, raw_ref, decay_ref, grad_ref, part_ref, paux_ref,
+    dx_ref, dbc_ref, draw_ref, out_ref,
+    dy_ref, own_part, own_aux, in_part, in_aux, sum_part, sum_aux, far_part, far_aux,
+    own_sem, dy_send, dy_recv, near_send, near_recv, far_send, far_recv,
 ):
+    chips = tm // 2
+    me = lax.axis_index("tm")
+    core = lax.rem(me, 2)
+    chip = lax.div(me, 2)
+    partner = me + 1 - 2 * core
+    own = [pltpu.make_async_copy(grad_ref.at[me], dy_ref.at[me], own_sem.at[0, 0])]
+    kinds = (
+        (part_ref, own_part, in_part, sum_part, far_part),
+        (paux_ref, own_aux, in_aux, sum_aux, far_aux),
+    )
+    for k, (src, mine, _, _, _) in enumerate(kinds):
+        for q in range(chips):
+            own.append(pltpu.make_async_copy(src.at[2 * q + core], mine.at[q], own_sem.at[k + 1, q]))
+    for copy in own:
+        copy.start()
+    greet_all(me, tm)
+    sends, nears = [], []
+    for k, (src, _, near, _, _) in enumerate(kinds):
+        for q in range(chips):
+            nears.append(
+                remote(
+                    src.at[2 * q + 1 - core], near.at[q], near_send.at[k, q], near_recv.at[k, q],
+                    partner,
+                )
+            )
+            nears[-1].start()
+    for d in range(1, tm):
+        peer = lax.rem(me + d, tm)
+        sends.append(
+            remote(grad_ref.at[peer], dy_ref.at[me], dy_send.at[d], dy_recv.at[me], peer)
+        )
+        sends[-1].start()
+    for copy in own + nears:
+        copy.wait()
+    for k, (_, mine, near, total, far) in enumerate(kinds):
+        for d in range(1, chips):
+            q = lax.rem(chip + d, chips)
+            total[q] = (mine[q].astype(F32) + near[q].astype(F32)).astype(BF16)
+            sends.append(
+                remote(
+                    total.at[q], far.at[chip], far_send.at[k, d], far_recv.at[k, chip],
+                    2 * q + core,
+                )
+            )
+            sends[-1].start()
+    for d in range(1, tm):
+        got = lax.rem(me + d, tm)
+        remote(grad_ref.at[got], dy_ref.at[got], dy_send.at[d], dy_recv.at[got], got).wait_recv()
+
     length = x_ref.shape[0]
     n = bc_ref.shape[1] // 4
     mask = jnp.where(iota((length, length), 0) >= iota((length, length), 1), 1.0, 0.0)
@@ -106,10 +230,26 @@
             dxs.append(mm(m.astype(BF16), gp, 0, 0))
         dx_ref[:, at : at + LANES] = jnp.where(first, dxs[0], dxs[1]).astype(BF16)
     draw = step_grad(row_sums, col_sums, raw, step, decay_row, mask)
-    draw_ref[...] = draw[:, :nheads].astype(BF16)
+    draw_ref[:, :nheads] = draw[:, :nheads].astype(BF16)
     dgb = (dgram * mask).astype(BF16)
     dbc_ref[:, :n] = mm(dgb, c, 0, 0).astype(BF16)
-    dbc_ref[:, n:] = mm(dgb, b).astype(BF16)
+    dbc_ref[:, n : 2 * n] = mm(dgb, b).astype(BF16)
+
+    totals = []
+    for k, (_, mine, near, total, far) in enumerate(kinds):
+        value = mine[chip].astype(F32) + near[chip].astype(F32)
+        for d in range(1, chips):
+            q = lax.rem(chip + d, chips)
+            remote(
+                total.at[q], far.at[q], far_send.at[k, d], far_recv.at[k, q], 2 * q + core
+            ).wait_recv()
+            value = value + far[q].astype(F32)
+        totals.append(value.astype(BF16))
+    out_ref[...] = totals[0]
+    dbc_ref[:, 2 * n :] = totals[1][:, : 2 * n]
+    draw_ref[:, nheads:] = totals[1][:, 2 * n :]
+    for copy in sends:
+        copy.wait_send()
 
 
 def temporal_kernel(
@@ -187,8 +327,16 @@
 
 
 VMEM = pl.BlockSpec(memory_space=pltpu.VMEM)
+ANY = pl.BlockSpec(memory_space=pl.ANY)
 SMEM = pl.BlockSpec(memory_space=pltpu.SMEM)
-PARAMS = pltpu.CompilerParams(vmem_limit_bytes=48 * 1024 * 1024)
+LIMIT = 48 * 1024 * 1024
+PARAMS = pltpu.CompilerParams(vmem_limit_bytes=LIMIT)
+
+
+def talking(number):
+    return pltpu.CompilerParams(
+        vmem_limit_bytes=LIMIT, collective_id=number, has_side_effects=True
+    )
 
 
 def on_device(x_inner, bc_inputs, step_raw, decay_rate, skip_gain, w_out, grad_out, tm):
@@ -201,27 +349,29 @@
     x, bc, raw = x_inner[0], bc_inputs[0], step_raw[0]
     decay_pad = jnp.pad(decay_rate, ((0, 0), (0, LANES - nheads)))
     aux = jnp.concatenate([bc[:, n2:], raw[:, nheads:]], axis=1)
-    aux_all = lax.all_gather(aux, "tm", axis=0)
-    go_all = lax.all_gather(grad_out[0], "tm", axis=0)
-
-    spatial = pl.pallas_call(
-        functools.partial(forward_kernel, nheads, chunk),
-        out_shape=jax.ShapeDtypeStruct((tm, patches, chunk), BF16),
-        in_specs=[VMEM] * 4,
-        out_specs=VMEM,
-        compiler_params=PARAMS,
+    auxw = aux.shape[1]
+
+    spatial_here, go_all, aux_all = pl.pallas_call(
+        functools.partial(forward_kernel, nheads, chunk, tm),
+        out_shape=(
+            jax.ShapeDtypeStruct((tm, patches, chunk), BF16),
+            jax.ShapeDtypeStruct((tm, patches, model), BF16),
+            jax.ShapeDtypeStruct((tm, patches, auxw), BF16),
+        ),
+        in_specs=[VMEM] * 4 + [ANY] * 2,
+        out_specs=(ANY, ANY, ANY),
+        scratch_shapes=[pltpu.VMEM((tm, patches, chunk), BF16), DMA((3,))] + [DMA((tm,))] * 6,
+        compiler_params=talking(0),
         name="spatial_forward",
         cost_estimate=pl.CostEstimate(
             flops=6 * patches * patches * inner, bytes_accessed=4 * patches * inner,
             transcendentals=patches * patches * nheads,
         ),
-    )(x, bc, raw, decay_pad)
-    spatial_here = lax.all_to_all(spatial, "tm", 0, 0, tiled=True)
+    )(x, bc, raw, decay_pad, grad_out[0], aux)
 
     rows = 32
     block = lambda width: pl.BlockSpec((tm, rows, width), lambda i: (0, i, 0))
     whole = pl.BlockSpec((chunk, model), lambda i: (0, 0))
-    auxw = aux.shape[1]
     base = (lax.axis_index("tm") * mine).astype(jnp.int32).reshape(1)
     grad_here, partial_out, partial_aux, grad_w = pl.pallas_call(
         functools.partial(temporal_kernel, nheads, mine, 16),
@@ -243,29 +393,30 @@
         ),
     )(base, decay_rate, skip_gain, spatial_here, go_all, aux_all, w_out)
 
-    grad_spatial = lax.all_to_all(grad_here, "tm", 0, 0, tiled=True)
-    mixed_out = lax.psum_scatter(partial_out, "tm", scatter_dimension=0, tiled=True)
-    aux_back = lax.psum_scatter(partial_aux, "tm", scatter_dimension=0, tiled=True)[0]
-
-    grad_x, grad_bc_s, grad_raw_s = pl.pallas_call(
-        functools.partial(backward_kernel, nheads, chunk),
+    chips = tm // 2
+    slots = lambda width: pltpu.VMEM((chips, patches, width), BF16)
+    grad_x, grad_bc, grad_step, mixed_out = pl.pallas_call(
+        functools.partial(backward_kernel, nheads, chunk, tm),
         out_shape=(
             jax.ShapeDtypeStruct((patches, inner), BF16),
-            jax.ShapeDtypeStruct((patches, n2), BF16),
-            jax.ShapeDtypeStruct((patches, nheads), BF16),
-        ),
-        in_specs=[VMEM] * 5,
-        out_specs=(VMEM, VMEM, VMEM),
-        compiler_params=PARAMS,
+            jax.ShapeDtypeStruct((patches, 2 * n2), BF16),
+            jax.ShapeDtypeStruct((patches, 2 * nheads), BF16),
+            jax.ShapeDtypeStruct((patches, model), BF16),
+        ),
+        in_specs=[VMEM] * 4 + [ANY] * 3,
+        out_specs=(VMEM,) * 4,
+        scratch_shapes=[pltpu.VMEM((tm, patches, chunk), BF16)]
+        + [slots(model), slots(auxw)] * 4
+        + [DMA((3, chips)), DMA((tm,)), DMA((tm,))]
+        + [DMA((2, chips))] * 4,
+        compiler_params=talking(1),
         name="spatial_backward",
         cost_estimate=pl.CostEstimate(
             flops=12 * patches * patches * inner, bytes_accessed=6 * patches * inner,
             transcendentals=patches * patches * nheads,
         ),
-    )(x, bc, raw, decay_pad, grad_spatial)
-    grad_bc = jnp.concatenate([grad_bc_s, aux_back[:, :n2]], axis=1)
-    grad_step = jnp.concatenate([grad_raw_s, aux_back[:, n2:]], axis=1)
-    return (mixed_out, grad_x[None], grad_bc[None], grad_step[None], grad_w)
+    )(x, bc, raw, decay_pad, grad_here, partial_out, partial_aux)
+    return (mixed_out[None], grad_x[None], grad_bc[None], grad_step[None], grad_w)
 
 
 def solution(mesh):

time: 180 us -> 163 us (0.906)
  Pallas kernels: 32.6 us -> 149 us
  waiting for transfers between devices: 63.6 us -> 0 us
  blocking collectives: 51.8 us -> 0 us
  between operations: 13.9 us -> 0.7 us
  starting transfers between devices: 10.5 us -> 0 us
  local copies, waits for them, and re-layouts: 6.44 us -> 12.4 us
    pallas_call x2, Pallas kernels: 11.6 us -> 128 us  [the longest x1 68.2 us: on_device(): pl.pallas_call(functools.partial(backward_kernel, nheads, chunk, tm), out...]
    reduce_scatter x2 -> x0, waiting for transfers between devices: 62.2 us -> none  [the longest x1 32.3 us: on_device(): lax.psum_scatter(partial_out, 'tm', scatter_dimension=0, tiled=True)]
    all_gather x1 -> x0, blocking collectives: 51.8 us -> none  [on_device(): aux_all = lax.all_gather(aux, 'tm', axis=0)]
    all_to_all x2 -> x0, starting transfers between devices: 10.3 us -> none  [the longest x1 6.32 us: on_device(): spatial_here = lax.all_to_all(spatial, 'tm', 0, 0, tiled=True)]
    unnamed x17 -> x23, local copies, waits for them, and re-layouts: 3.72 us -> 10.9 us
  transfers between devices with their start and end apart: 5 -> 0, of which waited for: 2 -> 0; matrix products, arithmetic and copies ran while one was open for 3% -> 0% of each run, Pallas kernels for 6% -> 0%
where the time goes in v1:
time: 163 us
  Pallas kernels  149 us (91%)
  local copies, waits for them, and re-layouts  12.4 us (8%)
    pallas_call x1, Pallas kernels, on_device(): pl.pallas_call(functools.partial(backward_kernel, nheads, chunk, tm), out...  68.2 us
    pallas_call x1, Pallas kernels, on_device(): pl.pallas_call(functools.partial(forward_kernel, nheads, chunk, tm), out_...  60.1 us
    pallas_call x1, Pallas kernels, on_device(): pl.pallas_call(functools.partial(temporal_kernel, nheads, mine, 16), grid...  21 us
    unnamed x23, local copies, waits for them, and re-layouts  10.9 us

profile of v1, /device:TPU:0, one launch (start us, length us, event | category | flops | bytes accessed | tf_op | source)
XLA Modules:
  0.0 162.5 jit_solution(4686186887592538384)
XLA Ops:
  0.6 0.7 pad.4.decay_ref
  1.3 0.8 slice.8
  2.1 0.9 copy.12
  3.0 0.1 slice.9
  3.1 0.0 copy-start
  3.1 1.1 copy-done
  4.2 0.0 copy-start.2
  4.3 0.9 copy-done.2
  5.1 0.0 copy-start.6
  5.1 1.0 copy-done.6
  6.1 60.1 %spatial_forward.1 = (bf16[8,192,256]{2,1,0:T(8,128)(2,1)S(1)}, bf16[8,192,1024]{2,1,0:T(8,128)(2,1)S(1)}, bf16[8,192,160]{2,1,0:T(8,128)(2,1)S(1)}) custom-call(bf16[192,2048]{1,0:T(8,128)(2,1)S(1)} %bitcast.9, bf16[192,256]{1,0:T(8,128)(2,1)S(1)} %bitcast.17, bf16[192,64]{1,0:T(8,128)(2,1)S(1)} %bitcast.13, f32[2,128]{1,0:T(2,128)S(1)} %pad.4.decay_ref, ...), custom_call_target="tpu_custom_call" | custom-call | flops 452984832 | bytes 1572864 | tf_op jit(solution)/shard_map/spatial_forward/pallas_call | solution.py:354
  66.3 0.0 copy-start.8
  66.3 1.6 copy-done.8
  67.9 0.0 copy-start.4
  67.9 0.7 copy-done.4
  68.6 0.0 copy-start.5
  68.6 1.0 copy-done.5
  69.6 0.0 copy-start.7
  69.6 0.7 copy-done.7
  70.3 0.0 copy-start.1
  70.3 0.0 copy-start.3
  70.3 21.0 %temporal.1 = (bf16[8,192,256]{2,1,0:T(8,128)(2,1)S(1)}, bf16[8,192,1024]{2,1,0:T(8,128)(2,1)}, bf16[8,192,160]{2,1,0:T(8,128)(2,1)S(1)}, f32[256,1024]{1,0:T(8,128)}) custom-call(s32[1]{0:T(128)} %bitcast.3.base_ref, f32[2,32]{1,0:T(2,128)S(1)} %copy-done.4, f32[32]{0:T(128)S(1)} %copy-done.7, bf16[8,192,256]{2,1,0:T(8,128)(2,1)S(1)} %get-tuple-element.16.x_ref, ...), custom_call_target="tpu_custom_call" | custom-call | flops 2415919104 | bytes 12582912 | tf_op jit(solution)/shard_map/temporal/pallas_call | solution.py:376
  91.3 0.0 copy-done.1
  91.3 0.0 copy-done.3
  91.3 68.2 %spatial_backward.1 = (bf16[192,2048]{1,0:T(8,128)(2,1)S(1)}, bf16[192,256]{1,0:T(8,128)(2,1)S(1)}, bf16[192,64]{1,0:T(8,128)(2,1)S(1)}, bf16[192,1024]{1,0:T(8,128)(2,1)S(1)}) custom-call(bf16[192,2048]{1,0:T(8,128)(2,1)S(1)} %bitcast.10, bf16[192,256]{1,0:T(8,128)(2,1)S(1)} %bitcast.18, bf16[192,64]{1,0:T(8,128)(2,1)S(1)} %bitcast.14, ...), custom_call_target="tpu_custom_call" | custom-call | flops 905969664 | bytes 2359296 | tf_op jit(solution)/shard_map/spatial_backward/pallas_call | solution.py:398
  159.5 0.7 copy.13
  160.2 0.7 copy.17
  161.0 0.9 copy.18
  161.9 0.6 copy.19
  (1 shorter events, 0.0 us)
Async XLA Ops:
  3.1 1.1 copy-start
  4.2 0.9 copy-start.2
  5.1 1.0 copy-start.6
  66.3 1.6 %copy-start.8 = (bf16[8,192,1024]{2,1,0:T(8,128)(2,1)}, bf16[8,192,1024]{2,1,0:T(8,128)(2,1)S(1)}, u32[]{:S(2)}) copy-start(bf16[8,192,1024]{2,1,0:T(8,128)(2,1)S(1)} %get-tuple-element.17.go_ref) | copy-start | bytes 9437188
  67.9 0.7 copy-start.4
  68.6 1.0 copy-start.5
  69.6 0.7 copy-start.7
  70.3 21.0 %copy-start.1 = (bf16[1,192,2048]{2,1,0:T(8,128)(2,1)S(1)}, bf16[1,192,2048]{2,1,0:T(8,128)(2,1)}, u32[]{:S(2)}) copy-start(bf16[1,192,2048]{2,1,0:T(8,128)(2,1)} %param.7) | copy-start | bytes 2359300
  70.3 21.0 %copy-start.3 = (bf16[1,192,256]{2,1,0:T(8,128)(2,1)S(1)}, bf16[1,192,256]{2,1,0:T(8,128)(2,1)}, u32[]{:S(2)}) copy-start(bf16[1,192,256]{2,1,0:T(8,128)(2,1)} %param.8) | copy-start | bytes 294916

commit v2 on v1

--- a/solution.py
+++ b/solution.py
@@ -33,6 +33,11 @@
 def picker(rows, base, count):
     r, c = iota((rows, LANES), 0), iota((rows, LANES), 1)
     return jnp.where((r == c + base) & (c < count), 1.0, 0.0).astype(BF16)
+
+
+def decay_lanes(decay_ref):
+    row = decay_ref[0:1, :]
+    return jnp.concatenate([row, jnp.zeros((1, LANES - row.shape[1]), F32)], axis=1)
 
 
 def steps_of(raw_bf, pick, decay_row, mask):
@@ -73,33 +78,44 @@
 
 def forward_kernel(
     nheads, chunk, tm,
-    x_ref, bc_ref, raw_ref, decay_ref, go_ref, aux_ref,
+    x_ref, bc_ref, raw_ref, decay_ref, go_ref,
     here_ref, go_all, aux_all,
-    out_ref, own_sem, sp_send, sp_recv, go_send, go_recv, aux_send, aux_recv,
+    out_ref, aux_vm, own_sem, sp_send, sp_recv, go_send, go_recv, aux_send, aux_recv,
 ):
     length = x_ref.shape[0]
     n = bc_ref.shape[1] // 4
     me = lax.axis_index("tm")
     core = lax.rem(me, 2)
     partner = me + 1 - 2 * core
+    chips, chip = tm // 2, lax.div(me, 2)
+    aux_vm[:, : 2 * n] = bc_ref[:, 2 * n :]
+    aux_vm[:, 2 * n :] = raw_ref[:, nheads:]
     own = [
         pltpu.make_async_copy(go_ref, go_all.at[me], own_sem.at[0]),
-        pltpu.make_async_copy(aux_ref, aux_all.at[me], own_sem.at[1]),
+        pltpu.make_async_copy(aux_vm, aux_all.at[me], own_sem.at[1]),
     ]
     for copy in own:
         copy.start()
     greet_all(me, tm)
-    gathers = ((go_ref, go_all, go_send, go_recv), (aux_ref, aux_all, aux_send, aux_recv))
-    sends = []
+    gathers = ((aux_vm, aux_all, aux_send, aux_recv), (go_ref, go_all, go_send, go_recv))
+
+    def hand_on(src, dst, send, recv, owner, right, left):
+        @pl.when(right)
+        def _():
+            remote(src, dst.at[owner], send.at[0, owner], recv.at[owner], me + 2).start()
+
+        @pl.when(left)
+        def _():
+            remote(src, dst.at[owner], send.at[1, owner], recv.at[owner], me - 2).start()
+
+        remote(src, dst.at[owner], send.at[2, owner], recv.at[owner], partner).start()
+
     for src, dst, send, recv in gathers:
-        for d in range(tm // 2):
-            peer = partner if d == 0 else lax.rem(me + 2 * d, tm)
-            sends.append(remote(src, dst.at[me], send.at[d], recv.at[me], peer))
-            sends[-1].start()
+        hand_on(src, dst, send, recv, me, chip < chips - 1, chip > 0)
 
     mask = jnp.where(iota((length, length), 0) >= iota((length, length), 1), 1.0, 0.0)
     pick = picker(raw_ref.shape[1], 0, nheads)
-    _, _, cum, step_t, cum_t = steps_of(raw_ref[...], pick, decay_ref[0:1, :], mask)
+    _, _, cum, step_t, cum_t = steps_of(raw_ref[...], pick, decay_lanes(decay_ref), mask)
     gram = mm(bc_ref[:, n : 2 * n], bc_ref[:, :n], 1, 1) * mask
     first = iota((length, LANES), 1) < LANES // 2
     for pair in range(nheads // 2):
@@ -113,6 +129,7 @@
             first, ys[0], ys[1]
         ).astype(BF16)
 
+    sends = []
     own.append(pltpu.make_async_copy(out_ref.at[me], here_ref.at[me], own_sem.at[2]))
     own[-1].start()
     for d in range(1, tm):
@@ -121,18 +138,39 @@
             remote(out_ref.at[peer], here_ref.at[me], sp_send.at[d], sp_recv.at[me], peer)
         )
         sends[-1].start()
-    for src, dst, send, recv in reversed(gathers):
-        for d in range(1, tm // 2):
-            got = lax.rem(me + 2 * d, tm)
-            remote(src, dst.at[got], send.at[0], recv.at[got], partner).wait_recv()
-            sends.append(
-                remote(dst.at[got], dst.at[got], send.at[tm // 2 + d], recv.at[got], partner)
-            )
-            sends[-1].start()
+    def passing(step, wait):
+        for sign in (-1, 1):
+            got = me + 2 * sign * step
+            here = (chip >= step) if sign < 0 else (chip < chips - step)
+            right = (chip < chips - 1) if sign < 0 else (chip < 0)
+            left = (chip < 0) if sign < 0 else (chip > 0)
+
+            @pl.when(here)
+            def _():
+                for src, dst, send, recv in gathers:
+                    wait(src, dst, send, recv, got, right, left)
+
+    def take(src, dst, send, recv, got, right, left):
+        remote(src, dst.at[got], send.at[2, got], recv.at[got], partner).wait_recv()
+        hand_on(dst.at[got], dst, send, recv, got, right, left)
+
+    def sent(src, dst, send, recv, got, right, left):
+        @pl.when(right)
+        def _():
+            remote(src, dst.at[got], send.at[0, got], recv.at[got], me + 2).wait_send()
+
+        @pl.when(left)
+        def _():
+            remote(src, dst.at[got], send.at[1, got], recv.at[got], me - 2).wait_send()
+
+        remote(src, dst.at[got], send.at[2, got], recv.at[got], partner).wait_send()
+
+    for step in range(1, chips):
+        passing(step, take)
     for src, dst, send, recv in gathers:
-        for d in range(tm // 2):
+        for d in range(chips):
             got = lax.rem(partner + 2 * d, tm)
-            remote(src, dst.at[got], send.at[0], recv.at[got], partner).wait_recv()
+            remote(src, dst.at[got], send.at[2, got], recv.at[got], partner).wait_recv()
     for d in range(1, tm):
         got = lax.rem(me + d, tm)
         remote(out_ref.at[got], here_ref.at[got], sp_send.at[d], sp_recv.at[got], got).wait_recv()
@@ -140,6 +178,10 @@
         copy.wait()
     for copy in sends:
         copy.wait_send()
+    for src, dst, send, recv in gathers:
+        sent(src, dst, send, recv, me, chip < chips - 1, chip > 0)
+    for step in range(1, chips):
+        passing(step, sent)
 
 
 def backward_kernel(
@@ -183,17 +225,37 @@
         sends[-1].start()
     for copy in own + nears:
         copy.wait()
-    for k, (_, mine, near, total, far) in enumerate(kinds):
-        for d in range(1, chips):
-            q = lax.rem(chip + d, chips)
+
+    def hop(k, q, side):
+        total, far = kinds[k][3], kinds[k][4]
+        return remote(
+            total.at[q], far.at[side, q], far_send.at[k, q], far_recv.at[k, side, q],
+            lax.rem(me + tm + 2 - 4 * side, tm),
+        )
+
+    def forward(q, side):
+        for k, (_, mine, near, total, far) in reversed(list(enumerate(kinds))):
             total[q] = (mine[q].astype(F32) + near[q].astype(F32)).astype(BF16)
-            sends.append(
-                remote(
-                    total.at[q], far.at[chip], far_send.at[k, d], far_recv.at[k, chip],
-                    2 * q + core,
-                )
-            )
-            sends[-1].start()
+
+            @pl.when((chip > 0) if side == 0 else (chip < chips - 1))
+            def _():
+                hop(k, q, side).wait_recv()
+                total[q] = (
+                    mine[q].astype(F32) + near[q].astype(F32) + far[side, q].astype(F32)
+                ).astype(BF16)
+
+            hop(k, q, side).start()
+
+    def round_of(step):
+        @pl.when(chips - 1 - step > chip)
+        def _():
+            forward(chips - 1 - step, 0)
+
+        @pl.when(step < chip)
+        def _():
+            forward(step, 1)
+
+    round_of(0)
     for d in range(1, tm):
         got = lax.rem(me + d, tm)
         remote(grad_ref.at[got], dy_ref.at[got], dy_send.at[d], dy_recv.at[got], got).wait_recv()
@@ -202,7 +264,7 @@
     n = bc_ref.shape[1] // 4
     mask = jnp.where(iota((length, length), 0) >= iota((length, length), 1), 1.0, 0.0)
     pick = picker(raw_ref.shape[1], 0, nheads)
-    decay_row = decay_ref[0:1, :]
+    decay_row = decay_lanes(decay_ref)
     raw, step, cum, step_t, cum_t = steps_of(raw_ref[...], pick, decay_row, mask)
     b, c = bc_ref[:, :n], bc_ref[:, n : 2 * n]
     gram = mm(c, b, 1, 1) * mask
@@ -213,6 +275,8 @@
     row_sums = jnp.zeros((length, LANES), F32)
     col_sums = jnp.zeros((LANES, length), F32)
     for pair in range(nheads // 2):
+        if pair and pair % (nheads // 2 // (chips - 1) + 1) == 0:
+            round_of(pair // (nheads // 2 // (chips - 1) + 1))
         at = pair * LANES
         xp = x_ref[:, at : at + LANES]
         gp = dy_ref[at // chunk, :, at % chunk : at % chunk + LANES]
@@ -235,21 +299,25 @@
     dbc_ref[:, :n] = mm(dgb, c, 0, 0).astype(BF16)
     dbc_ref[:, n : 2 * n] = mm(dgb, b).astype(BF16)
 
-    totals = []
-    for k, (_, mine, near, total, far) in enumerate(kinds):
-        value = mine[chip].astype(F32) + near[chip].astype(F32)
-        for d in range(1, chips):
-            q = lax.rem(chip + d, chips)
-            remote(
-                total.at[q], far.at[q], far_send.at[k, d], far_recv.at[k, q], 2 * q + core
-            ).wait_recv()
-            value = value + far[q].astype(F32)
-        totals.append(value.astype(BF16))
-    out_ref[...] = totals[0]
-    dbc_ref[:, 2 * n :] = totals[1][:, : 2 * n]
-    draw_ref[:, nheads:] = totals[1][:, 2 * n :]
+    for k, (_, mine, near, total, far) in reversed(list(enumerate(kinds))):
+        total[chip] = (mine[chip].astype(F32) + near[chip].astype(F32)).astype(BF16)
+        for side in range(2):
+            @pl.when((chip > 0) if side == 0 else (chip < chips - 1))
+            def _():
+                hop(k, chip, side).wait_recv()
+                total[chip] = (total[chip].astype(F32) + far[side, chip].astype(F32)).astype(BF16)
+
+    out_ref[...] = sum_part[chip]
+    other = sum_aux[chip]
+    dbc_ref[:, 2 * n :] = other[:, : 2 * n]
+    draw_ref[:, nheads:] = other[:, 2 * n :]
     for copy in sends:
         copy.wait_send()
+    for k in range(2):
+        for q in range(chips):
+            @pl.when(chip != q)
+            def _():
+                hop(k, q, 0).wait_send()
 
 
 def temporal_kernel(
@@ -274,13 +342,22 @@
     w = w_ref[...]
     go = go_ref[...].reshape(frames * patches, go_ref.shape[2])
     carried = mm(go, w, 1, 1).astype(BF16).reshape(frames, patches, width)
+    raws = mm(aux_ref[:, :, 2 * n :].reshape(frames * patches, nheads), pick)
+    steps = softplus(raws)
+    logs = (-steps * decay_row).reshape(frames, patches, LANES)
+    raws, steps = (v.reshape(frames, patches, LANES) for v in (raws, steps))
+    cums = [logs[0]]
+    for f in range(1, frames):
+        cums.append(cums[-1] + logs[f])
+    cums = jnp.stack(cums)
     for part in range(patches // group):
         sl = slice(part * group, (part + 1) * group)
         x = x_ref[:, sl, :].reshape(rows, width)
         g = carried[:, sl, :].reshape(rows, width)
         aux = aux_ref[:, sl, :].reshape(rows, aux_ref.shape[2])
         b, c = aux[:, :n], aux[:, n : 2 * n]
-        raw, step, cum, step_t, cum_t = steps_of(aux[:, 2 * n :], pick, decay_row, mask)
+        raw, step, cum = (v[:, sl, :].reshape(rows, LANES) for v in (raws, steps, cums))
+        step_t, cum_t = step.T, cum.T
         gram = mm(c, b, 1, 1) * mask
         dgram = jnp.zeros((rows, rows), F32)
         row_sums = jnp.zeros((rows, LANES), F32)
@@ -309,7 +386,13 @@
             dx = jnp.where(first, dxs[0], dxs[1]) + skip * gp.astype(F32)
             mixed_ref[:, sl, at : at + LANES] = y.astype(BF16).reshape(frames, group, LANES)
             dx_ref[:, sl, at : at + LANES] = dx.astype(BF16).reshape(frames, group, LANES)
-        draw = step_grad(row_sums, col_sums, raw, step, decay_row, mask)
+        col_sums = col_sums.T
+        ends = (row_sums - col_sums).reshape(frames, group, LANES)
+        later = [ends[frames - 1]]
+        for f in range(frames - 2, -1, -1):
+            later.append(later[-1] + ends[f])
+        later = jnp.stack(later[::-1]).reshape(rows, LANES)
+        draw = (col_sums / step - decay_row * later) / (1.0 + jnp.exp(-raw))
         placed = mm(draw.astype(BF16), pick, 1, 1)
         dgb = (dgram * mask).astype(BF16)
         shape = lambda v: v.astype(BF16).reshape(frames, group, v.shape[1])
@@ -329,7 +412,7 @@
 VMEM = pl.BlockSpec(memory_space=pltpu.VMEM)
 ANY = pl.BlockSpec(memory_space=pl.ANY)
 SMEM = pl.BlockSpec(memory_space=pltpu.SMEM)
-LIMIT = 48 * 1024 * 1024
+LIMIT = 60 * 1024 * 1024
 PARAMS = pltpu.CompilerParams(vmem_limit_bytes=LIMIT)
 
 
@@ -347,9 +430,7 @@
     chunk = inner // tm
     mine = nheads // tm
     x, bc, raw = x_inner[0], bc_inputs[0], step_raw[0]
-    decay_pad = jnp.pad(decay_rate, ((0, 0), (0, LANES - nheads)))
-    aux = jnp.concatenate([bc[:, n2:], raw[:, nheads:]], axis=1)
-    auxw = aux.shape[1]
+    auxw = n2 + nheads
 
     spatial_here, go_all, aux_all = pl.pallas_call(
         functools.partial(forward_kernel, nheads, chunk, tm),
@@ -358,18 +439,23 @@
             jax.ShapeDtypeStruct((tm, patches, model), BF16),
             jax.ShapeDtypeStruct((tm, patches, auxw), BF16),
         ),
-        in_specs=[VMEM] * 4 + [ANY] * 2,
+        in_specs=[VMEM] * 4 + [ANY],
         out_specs=(ANY, ANY, ANY),
-        scratch_shapes=[pltpu.VMEM((tm, patches, chunk), BF16), DMA((3,))] + [DMA((tm,))] * 6,
+        scratch_shapes=[
+            pltpu.VMEM((tm, patches, chunk), BF16),
+            pltpu.VMEM((patches, auxw), BF16),
+            DMA((3,)), DMA((tm,)), DMA((tm,)),
+            DMA((3, tm)), DMA((tm,)), DMA((3, tm)), DMA((tm,)),
+        ],
         compiler_params=talking(0),
         name="spatial_forward",
         cost_estimate=pl.CostEstimate(
             flops=6 * patches * patches * inner, bytes_accessed=4 * patches * inner,
             transcendentals=patches * patches * nheads,
         ),
-    )(x, bc, raw, decay_pad, grad_out[0], aux)
-
-    rows = 32
+    )(x, bc, raw, decay_rate, grad_out[0])
+
+    rows = 64 if patches % 64 == 0 else 32
     block = lambda width: pl.BlockSpec((tm, rows, width), lambda i: (0, i, 0))
     whole = pl.BlockSpec((chunk, model), lambda i: (0, 0))
     base = (lax.axis_index("tm") * mine).astype(jnp.int32).reshape(1)
@@ -406,16 +492,18 @@
         in_specs=[VMEM] * 4 + [ANY] * 3,
         out_specs=(VMEM,) * 4,
         scratch_shapes=[pltpu.VMEM((tm, patches, chunk), BF16)]
-        + [slots(model), slots(auxw)] * 4
+        + [slots(model), slots(auxw)] * 3
+        + [pltpu.VMEM((2, chips, patches, w), BF16) for w in (model, auxw)]
         + [DMA((3, chips)), DMA((tm,)), DMA((tm,))]
-        + [DMA((2, chips))] * 4,
+        + [DMA((2, chips))] * 3
+        + [DMA((2, 2, chips))],
         compiler_params=talking(1),
         name="spatial_backward",
         cost_estimate=pl.CostEstimate(
             flops=12 * patches * patches * inner, bytes_accessed=6 * patches * inner,
             transcendentals=patches * patches * nheads,
         ),
-    )(x, bc, raw, decay_pad, grad_here, partial_out, partial_aux)
+    )(x, bc, raw, decay_rate, grad_here, partial_out, partial_aux)
     return (mixed_out[None], grad_x[None], grad_bc[None], grad_step[None], grad_w)
 
 

time: 163 us -> 146 us (0.90); the launches traced: 163 us -> 143 us
  Pallas kernels: 149 us -> 134 us
  local copies, waits for them, and re-layouts: 12.4 us -> 8.37 us
    pallas_call x1, Pallas kernels: 68.2 us -> 61.3 us  [on_device(): pl.pallas_call(functools.partial(backward_kernel, nheads, chunk, tm), out...]
    pallas_call x1, Pallas kernels: 21 us -> 14.9 us  [on_device(): pl.pallas_call(functools.partial(temporal_kernel, nheads, mine, 16), grid...]
    unnamed x23 -> x5, local copies, waits for them, and re-layouts: 10.9 us -> 8.37 us
    pallas_call x1, Pallas kernels: 60.1 us -> 58.3 us  [on_device(): pl.pallas_call(functools.partial(forward_kernel, nheads, chunk, tm), out_...]
where the time goes in v2:
time: 146 us; the launch traced here: 143 us
  Pallas kernels  134 us (92%)
  local copies, waits for them, and re-layouts  8.37 us (6%)
    pallas_call x1, Pallas kernels, on_device(): pl.pallas_call(functools.partial(backward_kernel, nheads, chunk, tm), out...  61.3 us
    pallas_call x1, Pallas kernels, on_device(): pl.pallas_call(functools.partial(forward_kernel, nheads, chunk, tm), out_...  58.3 us
    pallas_call x1, Pallas kernels, on_device(): pl.pallas_call(functools.partial(temporal_kernel, nheads, mine, 16), grid...  14.9 us
    unnamed x5, local copies, waits for them, and re-layouts  8.37 us

profile of v2, /device:TPU:0, one launch (start us, length us, event | category | flops | bytes accessed | tf_op | source)
XLA Modules:
  0.0 143.5 jit_solution(3636583059848604088)
XLA Ops:
  0.6 1.5 %copy.12 = bf16[1,192,64]{2,1,0:T(8,128)(2,1)} copy(bf16[1,192,64]{1,2,0:T(8,128)(2,1)} %param.9) | data formatting | bytes 49152 | tf_op args[2]
  2.1 58.3 %spatial_forward.1 = (bf16[8,192,256]{2,1,0:T(8,128)(2,1)}, bf16[8,192,1024]{2,1,0:T(8,128)(2,1)}, bf16[8,192,160]{2,1,0:T(8,128)(2,1)}) custom-call(bf16[192,2048]{1,0:T(8,128)(2,1)} %bitcast.9, bf16[192,256]{1,0:T(8,128)(2,1)} %bitcast.16, bf16[192,64]{1,0:T(8,128)(2,1)} %bitcast.13, f32[2,32]{1,0:T(2,128)} %decay_ref.5, bf16[192,1024]{1,0:T(8,128)(2,1)} %bitcast.19), custom_call_target="tpu_custom_call" | custom-call | flops 452984832 | bytes 1572864 | tf_op jit(solution)/shard_map/spatial_forward/pallas_call | solution.py:435
  60.4 14.9 %temporal.1 = (bf16[8,192,256]{2,1,0:T(8,128)(2,1)}, bf16[8,192,1024]{2,1,0:T(8,128)(2,1)}, bf16[8,192,160]{2,1,0:T(8,128)(2,1)}, f32[256,1024]{1,0:T(8,128)}) custom-call(s32[1]{0:T(128)} %bitcast.3.base_ref, f32[2,32]{1,0:T(2,128)} %decay_ref.5, f32[32]{0:T(128)} %skip_ref.1, bf16[8,192,256]{2,1,0:T(8,128)(2,1)} %get-tuple-element.16.x_ref, ...), custom_call_target="tpu_custom_call" | custom-call | flops 2415919104 | bytes 12582912 | tf_op jit(solution)/shard_map/temporal/pallas_call | solution.py:462
  75.3 61.3 %spatial_backward.1 = (bf16[192,2048]{1,0:T(8,128)(2,1)}, bf16[192,256]{1,0:T(8,128)(2,1)}, bf16[192,64]{1,0:T(8,128)(2,1)}, bf16[192,1024]{1,0:T(8,128)(2,1)}) custom-call(bf16[192,2048]{1,0:T(8,128)(2,1)} %bitcast.10, bf16[192,256]{1,0:T(8,128)(2,1)} %bitcast.17, bf16[192,64]{1,0:T(8,128)(2,1)} %bitcast.14, f32[2,32]{1,0:T(2,128)} %decay_ref.5, ...), custom_call_target="tpu_custom_call" | custom-call | flops 905969664 | bytes 2359296 | tf_op jit(solution)/shard_map/spatial_backward/pallas_call | solution.py:484
  136.6 1.5 %copy.13 = bf16[1,192,64]{1,2,0:T(8,128)(2,1)} copy(bf16[1,192,64]{2,1,0:T(8,128)(2,1)} %bitcast.18) | data formatting | bytes 49152
  138.1 1.8 %copy.17 = bf16[1,192,1024]{2,1,0:T(8,128)(2,1)} copy(bf16[1,192,1024]{2,1,0:T(8,128)(2,1)} %bitcast.12) | data formatting | bytes 786432
  139.9 2.1 %copy.18 = bf16[1,192,2048]{2,1,0:T(8,128)(2,1)} copy(bf16[1,192,2048]{2,1,0:T(8,128)(2,1)} %bitcast.11) | data formatting | bytes 1572864
  142.0 1.5 %copy.19 = bf16[1,192,256]{2,1,0:T(8,128)(2,1)} copy(bf16[1,192,256]{2,1,0:T(8,128)(2,1)} %bitcast.15) | data formatting | bytes 196608

commit v3 on v2

--- a/solution.py
+++ b/solution.py
@@ -255,10 +255,13 @@
         def _():
             forward(step, 1)
 
+    inner_chip = (chip > 0) & (chip < chips - 1)
     round_of(0)
-    for d in range(1, tm):
-        got = lax.rem(me + d, tm)
-        remote(grad_ref.at[got], dy_ref.at[got], dy_send.at[d], dy_recv.at[got], got).wait_recv()
+
+    @pl.when(jnp.logical_not(inner_chip))
+    def _():
+        for step in range(1, chips - 1):
+            round_of(step)
 
     length = x_ref.shape[0]
     n = bc_ref.shape[1] // 4
@@ -271,12 +274,21 @@
     lane = iota((length, LANES), 1)
     first = lane < LANES // 2
     sub = iota((LANES, length), 0)
+    for d in range(1, tm):
+        got = lax.rem(me + d, tm)
+        remote(grad_ref.at[got], dy_ref.at[got], dy_send.at[d], dy_recv.at[got], got).wait_recv()
+
     dgram = jnp.zeros((length, length), F32)
     row_sums = jnp.zeros((length, LANES), F32)
     col_sums = jnp.zeros((LANES, length), F32)
     for pair in range(nheads // 2):
         if pair and pair % (nheads // 2 // (chips - 1) + 1) == 0:
-            round_of(pair // (nheads // 2 // (chips - 1) + 1))
+            rnd = pair // (nheads // 2 // (chips - 1) + 1)
+
+            @pl.when(inner_chip)
+            def _():
+                round_of(rnd)
+
         at = pair * LANES
         xp = x_ref[:, at : at + LANES]
         gp = dy_ref[at // chunk, :, at % chunk : at % chunk + LANES]
@@ -416,9 +428,9 @@
 PARAMS = pltpu.CompilerParams(vmem_limit_bytes=LIMIT)
 
 
-def talking(number):
+def talking(number, limit=LIMIT):
     return pltpu.CompilerParams(
-        vmem_limit_bytes=LIMIT, collective_id=number, has_side_effects=True
+        vmem_limit_bytes=limit, collective_id=number, has_side_effects=True
     )
 
 
@@ -497,7 +509,7 @@
         + [DMA((3, chips)), DMA((tm,)), DMA((tm,))]
         + [DMA((2, chips))] * 3
         + [DMA((2, 2, chips))],
-        compiler_params=talking(1),
+        compiler_params=talking(1, 40 * 1024 * 1024),
         name="spatial_backward",
         cost_estimate=pl.CostEstimate(
             flops=12 * patches * patches * inner, bytes_accessed=6 * patches * inner,

time: 146 us -> 145 us (level)
    unnamed x5 -> x19, local copies, waits for them, and re-layouts: 8.37 us -> 8.63 us
where the time goes in v3:
time: 145 us; the launch traced here: 143 us
  Pallas kernels  133 us (92%)
  local copies, waits for them, and re-layouts  8.63 us (6%)
    pallas_call x1, Pallas kernels, on_device(): pl.pallas_call(functools.partial(backward_kernel, nheads, chunk, tm), out...  60.1 us
    pallas_call x1, Pallas kernels, on_device(): pl.pallas_call(functools.partial(forward_kernel, nheads, chunk, tm), out_...  58.3 us
    pallas_call x1, Pallas kernels, on_device(): pl.pallas_call(functools.partial(temporal_kernel, nheads, mine, 16), grid...  15 us
    unnamed x19, local copies, waits for them, and re-layouts  8.63 us

profile of v3, /device:TPU:0, one launch (start us, length us, event | category | flops | bytes accessed | tf_op | source)
XLA Modules:
  0.0 142.7 jit_solution(16178354330213373632)
XLA Ops:
  0.6 1.5 %copy.12 = bf16[1,192,64]{2,1,0:T(8,128)(2,1)} copy(bf16[1,192,64]{1,2,0:T(8,128)(2,1)} %param.9) | data formatting | bytes 49152 | tf_op args[2]
  2.1 58.3 %spatial_forward.1 = (bf16[8,192,256]{2,1,0:T(8,128)(2,1)}, bf16[8,192,1024]{2,1,0:T(8,128)(2,1)}, bf16[8,192,160]{2,1,0:T(8,128)(2,1)}) custom-call(bf16[192,2048]{1,0:T(8,128)(2,1)} %bitcast.9, bf16[192,256]{1,0:T(8,128)(2,1)} %bitcast.16, bf16[192,64]{1,0:T(8,128)(2,1)} %bitcast.13, f32[2,32]{1,0:T(2,128)} %decay_ref.5, bf16[192,1024]{1,0:T(8,128)(2,1)} %bitcast.19), custom_call_target="tpu_custom_call" | custom-call | flops 452984832 | bytes 1572864 | tf_op jit(solution)/shard_map/spatial_forward/pallas_call | solution.py:447
  60.4 0.0 copy-start.1
  60.4 0.0 copy-start.4
  60.4 0.0 copy-start.5
  60.4 0.0 copy-start.6
  60.4 15.0 %temporal.1 = (bf16[8,192,256]{2,1,0:T(8,128)(2,1)}, bf16[8,192,1024]{2,1,0:T(8,128)(2,1)}, bf16[8,192,160]{2,1,0:T(8,128)(2,1)}, f32[256,1024]{1,0:T(8,128)}) custom-call(s32[1]{0:T(128)} %bitcast.3.base_ref, f32[2,32]{1,0:T(2,128)} %decay_ref.5, f32[32]{0:T(128)} %skip_ref.1, bf16[8,192,256]{2,1,0:T(8,128)(2,1)} %get-tuple-element.16.x_ref, ...), custom_call_target="tpu_custom_call" | custom-call | flops 2415919104 | bytes 12582912 | tf_op jit(solution)/shard_map/temporal/pallas_call | solution.py:474
  75.4 0.0 copy-done.1
  75.4 0.0 copy-done.4
  75.4 0.0 copy-done.5
  75.4 0.0 copy-done.6
  75.5 0.0 copy-start
  75.5 1.9 %copy-done = bf16[8,192,1024]{2,1,0:T(8,128)(2,1)S(1)} copy-done((bf16[8,192,1024]{2,1,0:T(8,128)(2,1)S(1)}, bf16[8,192,1024]{2,1,0:T(8,128)(2,1)}, u32[]{:S(2)}) %copy-start) | copy-done | bytes 3145752
  77.3 0.0 copy-start.2
  77.4 1.1 copy-done.2
  78.5 0.0 copy-start.3
  78.5 1.1 copy-done.3
  79.6 60.1 %spatial_backward.1 = (bf16[192,2048]{1,0:T(8,128)(2,1)S(1)}, bf16[192,256]{1,0:T(8,128)(2,1)S(1)}, bf16[192,64]{1,0:T(8,128)(2,1)S(1)}, bf16[192,1024]{1,0:T(8,128)(2,1)S(1)}) custom-call(bf16[192,2048]{1,0:T(8,128)(2,1)S(1)} %bitcast.10, bf16[192,256]{1,0:T(8,128)(2,1)S(1)} %bitcast.17, bf16[192,64]{1,0:T(8,128)(2,1)S(1)} %bitcast.14, ...), custom_call_target="tpu_custom_call" | custom-call | flops 905969664 | bytes 2359296 | tf_op jit(solution)/shard_map/spatial_backward/pallas_call | solution.py:496
  139.7 0.7 copy.13
  140.5 0.7 copy.17
  141.2 0.9 copy.18
  142.1 0.6 copy.19
Async XLA Ops:
  60.4 15.0 %copy-start.1 = (bf16[1,192,2048]{2,1,0:T(8,128)(2,1)S(1)}, bf16[1,192,2048]{2,1,0:T(8,128)(2,1)}, u32[]{:S(2)}) copy-start(bf16[1,192,2048]{2,1,0:T(8,128)(2,1)} %param.7) | copy-start | bytes 2359300
  60.4 15.0 %copy-start.4 = (bf16[1,192,64]{2,1,0:T(8,128)(2,1)S(1)}, bf16[1,192,64]{2,1,0:T(8,128)(2,1)}, u32[]{:S(2)}) copy-start(bf16[1,192,64]{2,1,0:T(8,128)(2,1)} %copy.12) | copy-start | bytes 73732
  60.4 15.0 %copy-start.5 = (bf16[1,192,256]{2,1,0:T(8,128)(2,1)S(1)}, bf16[1,192,256]{2,1,0:T(8,128)(2,1)}, u32[]{:S(2)}) copy-start(bf16[1,192,256]{2,1,0:T(8,128)(2,1)} %param.8) | copy-start | bytes 294916
  60.4 15.0 %copy-start.6 = (f32[2,32]{1,0:T(2,128)S(1)}, f32[2,32]{1,0:T(2,128)}, u32[]{:S(2)}) copy-start(f32[2,32]{1,0:T(2,128)} %decay_ref.5) | copy-start | bytes 772
  75.5 1.9 %copy-start = (bf16[8,192,1024]{2,1,0:T(8,128)(2,1)S(1)}, bf16[8,192,1024]{2,1,0:T(8,128)(2,1)}, u32[]{:S(2)}) copy-start(bf16[8,192,1024]{2,1,0:T(8,128)(2,1)} %get-tuple-element.20.part_ref) | copy-start | bytes 9437188
  77.3 1.1 copy-start.2
  78.5 1.1 copy-start.3
